TPU v7x, 32 devices: a whole 2x2x4 slice. The times are simulated.
32 devices in a mesh: rows: 16 (over z, x, core), seq: 2 (over y).
Axes of the slice: x: 2, y: 2, z: 4, core: 2. Of those that a mesh axis runs over, the one named last changes fastest.
Arguments:
- block_input: bfloat16 [64, 2048, 768], P('rows', 'seq'), may hold values from -6 to 6
- segment_ids: int32 [64, 2048], P('rows', 'seq'), may hold values from 0 to 3, as said below
- norm1_gain: float32 [768], replicated, may hold values from 0.1 to 1.9
- norm1_shift: float32 [768], replicated, may hold values from -3 to 3
- qkv_weight: bfloat16 [768, 2304], replicated, may hold values from -0.21875 to 0.21875
- qv_bias: float32 [1536], replicated, may hold values from -3 to 3
- proj_weight: bfloat16 [768, 768], replicated, may hold values from -6 to 6
- proj_bias: float32 [768], replicated, may hold values from -3 to 3
- norm2_gain: float32 [768], replicated, may hold values from 0.1 to 1.9
- norm2_shift: float32 [768], replicated, may hold values from -3 to 3
- fc_weight: bfloat16 [768, 3072], replicated, may hold values from -0.21875 to 0.21875
- fc_bias: float32 [3072], replicated, may hold values from -3 to 3
- out_weight: bfloat16 [3072, 768], replicated, may hold values from -0.3125 to 0.3125
- out_bias: float32 [768], replicated, may hold values from -3 to 3
- out_cotangent: bfloat16 [64, 2048, 768], P('rows', 'seq'), may hold values from -6 to 6
Outputs:
- layer_output: bfloat16 [64, 2048, 768], P('rows', 'seq')
- input_grad: float32 [64, 2048, 768], P('rows', 'seq')
- grad_norm1_gain: float32 [768], replicated
- grad_norm1_shift: float32 [768], replicated
- grad_qkv_weight: float32 [768, 2304], replicated
- grad_qv_bias: float32 [1536], replicated
- grad_proj_weight: float32 [768, 768], replicated
- grad_proj_bias: float32 [768], replicated
- grad_norm2_gain: float32 [768], replicated
- grad_norm2_shift: float32 [768], replicated
- grad_fc_weight: float32 [768, 3072], replicated
- grad_fc_bias: float32 [3072], replicated
- grad_out_weight: float32 [3072, 768], replicated
- grad_out_bias: float32 [768], replicated
Inputs may be any that keep to these rules, and one draw needn't show every extreme that they name: `segment_ids`: along each row the ids never fall; every row holds documents 0, 1 and 2 in that order, then padding marked 3 that ends the row.
All inputs are finite; a program needn't handle non-finite values.
Results may differ from a plain program's by a relative error of at most 0.02.
Values may be sent and summed in bfloat16 or wider, within the bound.
A program may use at most 576 MiB of HBM per device.

v0:
```python
from functools import partial

import jax
import jax.numpy as jnp
from jax import lax
from jax.sharding import PartitionSpec as P

HEADS = 12
HEAD_DIM = 64


BRANCH = 12 ** (-0.5)
EPSILON = 1e-05
PADDING = 3.0
NEGATIVE = -1e30
block_keys = 256


def layer_norm(values, scale_gain, shift_bias):
    center = values - jnp.mean(values, axis=-1, keepdims=True)
    variance = jnp.mean(center * center, axis=-1, keepdims=True)
    return center * lax.rsqrt(variance + EPSILON) * scale_gain + shift_bias


def allowed_pairs(query_segments, key_segments, query_slots, key_slots):
    same_doc = query_segments[:, :, None] == key_segments[:, None, :]
    causal = key_slots[None, None, :] <= query_slots[None, :, None]
    itself = key_slots[None, None, :] == query_slots[None, :, None]
    unpadded = key_segments[:, None, :] != PADDING
    return (same_doc & causal & (unpadded | itself))[:, None]


def split_heads(block_rows):
    return block_rows.reshape(block_rows.shape[0], block_rows.shape[1], HEADS, HEAD_DIM)


def fold_blocks(block_step, running, piece_tuple):
    piece_len = piece_tuple[0].shape[1]

    def one_block(block_index, held_state):
        offset = block_index * block_keys
        sub_tuple = tuple(
            (lax.dynamic_slice_in_dim(member, offset, block_keys, 1) for member in piece_tuple)
        )
        return block_step(held_state, sub_tuple, offset)

    return lax.fori_loop(0, piece_len // block_keys, one_block, running)


def keep_same(running):
    return running


def local(
    block_input,
    segment_ids,
    norm1_gain,
    norm1_shift,
    qkv_weight,
    qv_bias,
    proj_weight,
    proj_bias,
    norm2_gain,
    norm2_shift,
    fc_weight,
    fc_bias,
    out_weight,
    out_bias,
    out_cotangent,
):
    row_count, local_len, model_width = block_input.shape
    tokens = row_count * local_len
    full_len = local_len * lax.axis_size("seq")
    my_first = lax.axis_index("seq") * local_len
    query_slots = my_first + jnp.arange(local_len)
    my_segments = segment_ids.astype(jnp.bfloat16)
    my_seg_float = segment_ids.astype(jnp.float32)
    score_scale = HEAD_DIM ** (-0.5)
    inputs = block_input.astype(jnp.float32).reshape(tokens, model_width)
    normed_one = layer_norm(inputs, norm1_gain, norm1_shift).astype(jnp.bfloat16)
    mixed_qkv = jnp.dot(normed_one, qkv_weight, preferred_element_type=jnp.float32)
    query_flat = (
        (mixed_qkv[:, :model_width] + qv_bias[:model_width])
        .astype(jnp.bfloat16)
        .reshape(row_count, local_len, model_width)
    )
    key_rows = (
        mixed_qkv[:, model_width : 2 * model_width]
        .astype(jnp.bfloat16)
        .reshape(row_count, local_len, model_width)
    )
    value_rows = (
        (mixed_qkv[:, 2 * model_width :] + qv_bias[model_width:])
        .astype(jnp.bfloat16)
        .reshape(row_count, local_len, model_width)
    )
    queries = split_heads(query_flat)

    def attend_block(running, sub_tuple, first_slot):
        key_piece, value_piece, seg_piece = sub_tuple
        piece_len = key_piece.shape[1]
        key_slots = first_slot + jnp.arange(piece_len)
        seg_float = seg_piece.astype(jnp.float32)
        skipped = (first_slot > my_first + local_len - 1) | (
            jnp.max(seg_float) < jnp.min(my_seg_float)
        )

        def attend_update(state):
            running_max, running_sum, running_out = state
            scores = (
                jnp.einsum(
                    "rqhd,rkhd->rhqk",
                    queries,
                    split_heads(key_piece),
                    preferred_element_type=jnp.float32,
                )
                * score_scale
            )
            allowed = allowed_pairs(my_seg_float, seg_float, query_slots, key_slots)
            masked = jnp.where(allowed, scores, NEGATIVE)
            new_max = jnp.maximum(running_max, jnp.max(masked, axis=-1))
            prob_block = jnp.where(allowed, jnp.exp(scores - new_max[..., None]), 0.0)
            factor = jnp.exp(running_max - new_max)
            new_sum = running_sum * factor + jnp.sum(prob_block, axis=-1)
            added_part = jnp.einsum(
                "rhqk,rkhd->rqhd",
                prob_block.astype(jnp.bfloat16),
                split_heads(value_piece),
                preferred_element_type=jnp.float32,
            )
            new_out = running_out * jnp.transpose(factor, (0, 2, 1))[..., None] + added_part
            return (new_max, new_sum, new_out)

        return lax.cond(skipped, keep_same, attend_update, running)

    start_state = (
        jnp.full((row_count, HEADS, local_len), NEGATIVE, jnp.float32),
        jnp.zeros((row_count, HEADS, local_len), jnp.float32),
        jnp.zeros((row_count, local_len, HEADS, HEAD_DIM), jnp.float32),
    )
    running_max, running_sum, running_out = fold_blocks(
        attend_block,
        start_state,
        (
            lax.all_gather(key_rows, "seq", axis=1, tiled=True),
            lax.all_gather(value_rows, "seq", axis=1, tiled=True),
            lax.all_gather(my_segments, "seq", axis=1, tiled=True),
        ),
    )
    log_total = running_max + jnp.log(running_sum)
    attended_heads = running_out / jnp.transpose(running_sum, (0, 2, 1))[..., None]
    attended_low = attended_heads.reshape(tokens, model_width).astype(jnp.bfloat16)
    branch_one = jnp.dot(attended_low, proj_weight, preferred_element_type=jnp.float32) + proj_bias
    middle = inputs + BRANCH * branch_one
    normed_two = layer_norm(middle, norm2_gain, norm2_shift).astype(jnp.bfloat16)
    hidden_pre = jnp.dot(normed_two, fc_weight, preferred_element_type=jnp.float32) + fc_bias
    hidden_act = jax.nn.gelu(hidden_pre, approximate=True).astype(jnp.bfloat16)
    branch_two = jnp.dot(hidden_act, out_weight, preferred_element_type=jnp.float32) + out_bias
    layer_output = (
        (middle + BRANCH * branch_two)
        .astype(jnp.bfloat16)
        .reshape(row_count, local_len, model_width)
    )
    flat_cot = out_cotangent.reshape(tokens, model_width).astype(jnp.float32)
    grad_two = (BRANCH * flat_cot).astype(jnp.bfloat16)
    grad_out_weight = jnp.einsum(
        "tf,td->fd", hidden_act, grad_two, preferred_element_type=jnp.float32
    )
    grad_out_bias = jnp.sum(grad_two.astype(jnp.float32), axis=0)
    grad_act = jnp.einsum("td,fd->tf", grad_two, out_weight, preferred_element_type=jnp.float32)
    gelu_value, gelu_pull = jax.vjp(partial(jax.nn.gelu, approximate=True), hidden_pre)
    grad_pre = gelu_pull(grad_act)[0].astype(jnp.bfloat16)
    grad_fc_weight = jnp.einsum(
        "td,tf->df", normed_two, grad_pre, preferred_element_type=jnp.float32
    )
    grad_fc_bias = jnp.sum(grad_pre.astype(jnp.float32), axis=0)
    grad_normed_two = jnp.einsum(
        "tf,df->td", grad_pre, fc_weight, preferred_element_type=jnp.float32
    )
    norm_value, norm_pull = jax.vjp(layer_norm, middle, norm2_gain, norm2_shift)
    grad_inner, grad_norm2_gain, grad_norm2_shift = norm_pull(grad_normed_two)
    grad_middle = flat_cot + grad_inner
    grad_one = (BRANCH * grad_middle).astype(jnp.bfloat16)
    grad_proj_weight = jnp.einsum(
        "td,te->de", attended_low, grad_one, preferred_element_type=jnp.float32
    )
    grad_proj_bias = jnp.sum(grad_one.astype(jnp.float32), axis=0)
    grad_attended_flat = (
        jnp.einsum("te,de->td", grad_one, proj_weight, preferred_element_type=jnp.float32)
        .astype(jnp.bfloat16)
        .reshape(row_count, local_len, model_width)
    )
    grad_attended = split_heads(grad_attended_flat)
    grad_delta = jnp.einsum("rqhd,rqhd->rhq", grad_attended.astype(jnp.float32), attended_heads)

    def back_block(running, sub_tuple, first_slot):
        key_piece, value_piece, seg_piece = sub_tuple
        piece_len = key_piece.shape[1]
        key_slots = first_slot + jnp.arange(piece_len)
        seg_float = seg_piece.astype(jnp.float32)
        skipped = (first_slot > my_first + local_len - 1) | (
            jnp.max(seg_float) < jnp.min(my_seg_float)
        )

        def back_update(state):
            grad_query, grad_full = state
            key_heads = split_heads(key_piece)
            value_heads = split_heads(value_piece)
            scores = (
                jnp.einsum(
                    "rqhd,rkhd->rhqk", queries, key_heads, preferred_element_type=jnp.float32
                )
                * score_scale
            )
            allowed = allowed_pairs(my_seg_float, seg_float, query_slots, key_slots)
            prob_block = jnp.where(allowed, jnp.exp(scores - log_total[..., None]), 0.0)
            grad_probs = jnp.einsum(
                "rqhd,rkhd->rhqk", grad_attended, value_heads, preferred_element_type=jnp.float32
            )
            grad_scores = (score_scale * prob_block * (grad_probs - grad_delta[..., None])).astype(
                jnp.bfloat16
            )
            new_query = grad_query + jnp.einsum(
                "rhqk,rkhd->rqhd", grad_scores, key_heads, preferred_element_type=jnp.float32
            )
            grad_keys = jnp.einsum(
                "rhqk,rqhd->rkhd", grad_scores, queries, preferred_element_type=jnp.float32
            ).reshape(row_count, piece_len, model_width)
            grad_values = jnp.einsum(
                "rhqk,rqhd->rkhd",
                prob_block.astype(jnp.bfloat16),
                grad_attended,
                preferred_element_type=jnp.float32,
            ).reshape(row_count, piece_len, model_width)
            held_part = lax.dynamic_slice_in_dim(grad_full, first_slot, piece_len, 2)
            new_full = lax.dynamic_update_slice_in_dim(
                grad_full, held_part + jnp.stack((grad_keys, grad_values)), first_slot, 2
            )
            return (new_query, new_full)

        return lax.cond(skipped, keep_same, back_update, running)

    back_start = (
        jnp.zeros((row_count, local_len, HEADS, HEAD_DIM), jnp.float32),
        jnp.zeros((2, row_count, full_len, model_width), jnp.float32),
    )
    grad_query, grad_full = fold_blocks(
        back_block,
        back_start,
        (
            lax.all_gather(key_rows, "seq", axis=1, tiled=True),
            lax.all_gather(value_rows, "seq", axis=1, tiled=True),
            lax.all_gather(my_segments, "seq", axis=1, tiled=True),
        ),
    )
    grad_pairs = lax.psum_scatter(
        grad_full.astype(jnp.bfloat16), "seq", scatter_dimension=2, tiled=True
    ).astype(jnp.float32)
    grad_query_low = grad_query.reshape(row_count, local_len, model_width).astype(jnp.bfloat16)
    grad_key_low = grad_pairs[0].astype(jnp.bfloat16)
    grad_value_low = grad_pairs[1].astype(jnp.bfloat16)
    grad_qkv_low = jnp.concatenate((grad_query_low, grad_key_low, grad_value_low), axis=-1).reshape(
        tokens, 3 * model_width
    )
    grad_qkv_weight = jnp.einsum(
        "td,te->de", normed_one, grad_qkv_low, preferred_element_type=jnp.float32
    )
    grad_qv_bias = jnp.concatenate(
        (
            jnp.sum(grad_query_low.astype(jnp.float32), axis=(0, 1)),
            jnp.sum(grad_value_low.astype(jnp.float32), axis=(0, 1)),
        )
    )
    grad_normed_one = jnp.einsum(
        "te,de->td", grad_qkv_low, qkv_weight, preferred_element_type=jnp.float32
    )
    first_value, first_pull = jax.vjp(layer_norm, inputs, norm1_gain, norm1_shift)
    grad_first, grad_norm1_gain, grad_norm1_shift = first_pull(grad_normed_one)
    input_grad = (grad_middle + grad_first).reshape(row_count, local_len, model_width)
    local_grads = (
        grad_norm1_gain,
        grad_norm1_shift,
        grad_qkv_weight,
        grad_qv_bias,
        grad_proj_weight,
        grad_proj_bias,
        grad_norm2_gain,
        grad_norm2_shift,
        grad_fc_weight,
        grad_fc_bias,
        grad_out_weight,
        grad_out_bias,
    )
    shares = (
        lax.psum_scatter(
            local_grads[0].astype(jnp.bfloat16), "rows", scatter_dimension=0, tiled=True
        ).astype(jnp.float32),
        lax.psum_scatter(
            local_grads[1].astype(jnp.bfloat16), "rows", scatter_dimension=0, tiled=True
        ).astype(jnp.float32),
        lax.psum_scatter(
            local_grads[2].astype(jnp.bfloat16), "rows", scatter_dimension=0, tiled=True
        ).astype(jnp.float32),
        lax.psum_scatter(
            local_grads[3].astype(jnp.bfloat16), "rows", scatter_dimension=0, tiled=True
        ).astype(jnp.float32),
        lax.psum_scatter(
            local_grads[4].astype(jnp.bfloat16), "rows", scatter_dimension=0, tiled=True
        ).astype(jnp.float32),
        lax.psum_scatter(
            local_grads[5].astype(jnp.bfloat16), "rows", scatter_dimension=0, tiled=True
        ).astype(jnp.float32),
        lax.psum_scatter(
            local_grads[6].astype(jnp.bfloat16), "rows", scatter_dimension=0, tiled=True
        ).astype(jnp.float32),
        lax.psum_scatter(
            local_grads[7].astype(jnp.bfloat16), "rows", scatter_dimension=0, tiled=True
        ).astype(jnp.float32),
        lax.psum_scatter(
            local_grads[8].astype(jnp.bfloat16), "rows", scatter_dimension=0, tiled=True
        ).astype(jnp.float32),
        lax.psum_scatter(
            local_grads[9].astype(jnp.bfloat16), "rows", scatter_dimension=0, tiled=True
        ).astype(jnp.float32),
        lax.psum_scatter(
            local_grads[10].astype(jnp.bfloat16), "rows", scatter_dimension=0, tiled=True
        ).astype(jnp.float32),
        lax.psum_scatter(
            local_grads[11].astype(jnp.bfloat16), "rows", scatter_dimension=0, tiled=True
        ).astype(jnp.float32),
    )
    shares = (
        lax.psum(shares[0].astype(jnp.bfloat16), "seq").astype(jnp.float32),
        lax.psum(shares[1].astype(jnp.bfloat16), "seq").astype(jnp.float32),
        lax.psum(shares[2].astype(jnp.bfloat16), "seq").astype(jnp.float32),
        lax.psum(shares[3].astype(jnp.bfloat16), "seq").astype(jnp.float32),
        lax.psum(shares[4].astype(jnp.bfloat16), "seq").astype(jnp.float32),
        lax.psum(shares[5].astype(jnp.bfloat16), "seq").astype(jnp.float32),
        lax.psum(shares[6].astype(jnp.bfloat16), "seq").astype(jnp.float32),
        lax.psum(shares[7].astype(jnp.bfloat16), "seq").astype(jnp.float32),
        lax.psum(shares[8].astype(jnp.bfloat16), "seq").astype(jnp.float32),
        lax.psum(shares[9].astype(jnp.bfloat16), "seq").astype(jnp.float32),
        lax.psum(shares[10].astype(jnp.bfloat16), "seq").astype(jnp.float32),
        lax.psum(shares[11].astype(jnp.bfloat16), "seq").astype(jnp.float32),
    )
    totals = (
        lax.all_gather(shares[0].astype(jnp.bfloat16), "rows", axis=0, tiled=True).astype(
            jnp.float32
        ),
        lax.all_gather(shares[1].astype(jnp.bfloat16), "rows", axis=0, tiled=True).astype(
            jnp.float32
        ),
        lax.all_gather(shares[2].astype(jnp.bfloat16), "rows", axis=0, tiled=True).astype(
            jnp.float32
        ),
        lax.all_gather(shares[3].astype(jnp.bfloat16), "rows", axis=0, tiled=True).astype(
            jnp.float32
        ),
        lax.all_gather(shares[4].astype(jnp.bfloat16), "rows", axis=0, tiled=True).astype(
            jnp.float32
        ),
        lax.all_gather(shares[5].astype(jnp.bfloat16), "rows", axis=0, tiled=True).astype(
            jnp.float32
        ),
        lax.all_gather(shares[6].astype(jnp.bfloat16), "rows", axis=0, tiled=True).astype(
            jnp.float32
        ),
        lax.all_gather(shares[7].astype(jnp.bfloat16), "rows", axis=0, tiled=True).astype(
            jnp.float32
        ),
        lax.all_gather(shares[8].astype(jnp.bfloat16), "rows", axis=0, tiled=True).astype(
            jnp.float32
        ),
        lax.all_gather(shares[9].astype(jnp.bfloat16), "rows", axis=0, tiled=True).astype(
            jnp.float32
        ),
        lax.all_gather(shares[10].astype(jnp.bfloat16), "rows", axis=0, tiled=True).astype(
            jnp.float32
        ),
        lax.all_gather(shares[11].astype(jnp.bfloat16), "rows", axis=0, tiled=True).astype(
            jnp.float32
        ),
    )
    return (layer_output, input_grad) + tuple(totals)


def solution(mesh):
    in_specs = (
        P("rows", "seq", None),
        P("rows", "seq"),
        P(),
        P(),
        P(),
        P(),
        P(),
        P(),
        P(),
        P(),
        P(),
        P(),
        P(),
        P(),
        P("rows", "seq", None),
    )
    out_specs = (
        P("rows", "seq", None),
        P("rows", "seq", None),
        P(),
        P(),
        P(),
        P(),
        P(),
        P(),
        P(),
        P(),
        P(),
        P(),
        P(),
        P(),
    )
    return jax.shard_map(local, mesh=mesh, in_specs=in_specs, out_specs=out_specs, check_vma=False)
```

profile of v0, /device:TPU:0, one launch (start us, length us, event | category | flops | bytes accessed | tf_op | source)
XLA Modules:
  0.0 3318.9 jit_solution(8163676020602107736)
XLA Ops:
  125.2 88.6 %all-gather.7.cloned.1.call-done = bf16[4,2048,768]{1,2,0:T(8,128)(2,1)} async-done(((bf16[4,1024,768]{1,2,0:T(8,128)(2,1)}), bf16[4,2048,768]{1,2,0:T(8,128)(2,1)}) %all-gather.7.cloned.1.call-update) | async-done | bytes 12582928 | tf_op jit(solution)/shard_map/all_gather | solution.py:145
  213.8 154.7 %all-gather.9.cloned.1.call-done = bf16[4,2048,768]{1,2,0:T(8,128)(2,1)} async-done(((bf16[4,1024,768]{1,2,0:T(8,128)(2,1)}), bf16[4,2048,768]{1,2,0:T(8,128)(2,1)}) %all-gather.9.cloned.1.call-update) | async-done | bytes 12582928 | tf_op jit(solution)/shard_map/all_gather | solution.py:146
  376.4 357.1 %while.38 = (s32[]{:T(128)}, f32[4,12,1024]{2,1,0:T(8,128)}, f32[4,12,1024]{2,1,0:T(8,128)}, f32[4,1024,12,64]{1,3,2,0:T(8,128)}, s32[]{:T(128)}, /*index=5*/bf1...) while((s32[]{:T(128)}, f32[4,12,1024]{2,1,0:T(8,128)}, ...), condition=%wide.region_9.10_spmd.clone, body=%wide.region_3.9_spmd.clone.sunk | while | flops 3370799360 | bytes 228643376 | solution.py:47
  380.6 78.3 %conditional.6 = (f32[4,12,1024]{2,1,0:T(8,128)S(1)}, f32[4,12,1024]{2,1,0:T(8,128)}, f32[4,1024,12,64]{1,3,2,0:T(8,128)}) conditional(s32[]{:T(128)} %convert_element_type.398, (f32[4,1024]{1,0:T(4,128)S(1)}, f32[4,256]{1,0:T(4,128)}, s32[]{:T(128)}, s32[256]{0:T(256)}, s32[]{:T(128)}, /*index=5*/bf16[4,2048,768]{1,2,0:T(8,128)(2,1)}, s32[]{:T(128)}, ...), branch_computations={%region_5.7_spmd, %region_8.8_spmd} | conditional | flops 3370797312 | bytes 228238528 | solution.py:134
  463.9 78.3 %conditional.6 = (f32[4,12,1024]{2,1,0:T(8,128)S(1)}, f32[4,12,1024]{2,1,0:T(8,128)}, f32[4,1024,12,64]{1,3,2,0:T(8,128)}) conditional(s32[]{:T(128)} %convert_element_type.398, (f32[4,1024]{1,0:T(4,128)S(1)}, f32[4,256]{1,0:T(4,128)}, s32[]{:T(128)}, s32[256]{0:T(256)}, s32[]{:T(128)}, /*index=5*/bf16[4,2048,768]{1,2,0:T(8,128)(2,1)}, s32[]{:T(128)}, ...), branch_computations={%region_5.7_spmd, %region_8.8_spmd} | conditional | flops 3370797312 | bytes 228238528 | solution.py:134
  547.1 78.3 %conditional.6 = (f32[4,12,1024]{2,1,0:T(8,128)S(1)}, f32[4,12,1024]{2,1,0:T(8,128)}, f32[4,1024,12,64]{1,3,2,0:T(8,128)}) conditional(s32[]{:T(128)} %convert_element_type.398, (f32[4,1024]{1,0:T(4,128)S(1)}, f32[4,256]{1,0:T(4,128)}, s32[]{:T(128)}, s32[256]{0:T(256)}, s32[]{:T(128)}, /*index=5*/bf16[4,2048,768]{1,2,0:T(8,128)(2,1)}, s32[]{:T(128)}, ...), branch_computations={%region_5.7_spmd, %region_8.8_spmd} | conditional | flops 3370797312 | bytes 228238528 | solution.py:134
  630.3 78.3 %conditional.6 = (f32[4,12,1024]{2,1,0:T(8,128)S(1)}, f32[4,12,1024]{2,1,0:T(8,128)}, f32[4,1024,12,64]{1,3,2,0:T(8,128)}) conditional(s32[]{:T(128)} %convert_element_type.398, (f32[4,1024]{1,0:T(4,128)S(1)}, f32[4,256]{1,0:T(4,128)}, s32[]{:T(128)}, s32[256]{0:T(256)}, s32[]{:T(128)}, /*index=5*/bf16[4,2048,768]{1,2,0:T(8,128)(2,1)}, s32[]{:T(128)}, ...), branch_computations={%region_5.7_spmd, %region_8.8_spmd} | conditional | flops 3370797312 | bytes 228238528 | solution.py:134
  777.2 39.2 %multiply_convert_fusion = (bf16[4096,3072]{1,0:T(8,128)(2,1)}, f32[4096,3072]{1,0:T(8,128)}) fusion(f32[3072]{0:T(1024)} %param.34, bf16[768,3072]{1,0:T(8,128)(2,1)} %param.33, f32[4096,768]{1,0:T(8,128)} %get-tuple-element.1133, f32[768]{0:T(1024)} %param.32, f32[768]{0:T(1024)} %param.31, f32[4096]{0:T(1024)} %fusion.55, ...), kind=kOutput, calls=%fused_computation.57 | convolution fusion | flops 19468910592 | bytes 92850176 | tf_op jit(solution)/shard_map/dot_general | solution.py:156
  816.3 57.4 %fusion.69 = (bf16[3072]{0:T(1024)(128)(2,1)}, bf16[4096,3072]{1,0:T(8,128)(2,1)}) fusion(f32[4096,3072]{1,0:T(8,128)} %get-tuple-element.1135, f32[3072]{0:T(1024)} %param.34, bf16[4096,768]{1,0:T(8,128)(2,1)} %fusion.35, bf16[3072,768]{1,0:T(8,128)(2,1)} %param.35), kind=kOutput, calls=%fused_computation.136 | convolution fusion | flops 19604172800 | bytes 86525952 | tf_op jit(solution)/shard_map/td,fd->tf/dot_general | solution.py:170
  873.7 32.1 multiply_reduce_fusion.1
  1009.3 551.1 %while.39 = (s32[]{:T(128)}, f32[4,1024,12,64]{1,3,2,0:T(8,128)}, f32[2,4,2048,768]{2,3,1,0:T(8,128)}, s32[]{:T(128)}, bf16[4,2048]{1,0:T(4,128)(2,1)}, /*index=...) while((s32[]{:T(128)}, f32[4,1024,12,64]{1,3,2,0:T(8,128)}, ...), condition=%wide.region_18.19_spmd.clone, body=%wide.region_14.18_spmd.clone.sunk | while | flops 8202489856 | bytes 317837760 | solution.py:47
  1014.0 129.1 %conditional.7 = ((f32[4,1024,12,64]{1,3,2,0:T(8,128)}, f32[2,4,2048,768]{2,3,1,0:T(8,128)})) conditional(s32[]{:T(128)} %convert_element_type.400, (f32[4,1024]{1,0:T(4,128)S(1)}, f32[4,256]{1,0:T(4,128)}, s32[]{:T(128)}, s32[256]{0:T(256)}, s32[]{:T(128)}, /*index=5*/bf16[4,2048,768]{1,2,0:T(8,128)(2,1)}, s32[]{:T(128)}, ...), branch_computations={%region_16.16_spmd, %region_17.17_spmd} | conditional | flops 8202487808 | bytes 317826112 | solution.py:241
  1147.3 129.1 %conditional.7 = ((f32[4,1024,12,64]{1,3,2,0:T(8,128)}, f32[2,4,2048,768]{2,3,1,0:T(8,128)})) conditional(s32[]{:T(128)} %convert_element_type.400, (f32[4,1024]{1,0:T(4,128)S(1)}, f32[4,256]{1,0:T(4,128)}, s32[]{:T(128)}, s32[256]{0:T(256)}, s32[]{:T(128)}, /*index=5*/bf16[4,2048,768]{1,2,0:T(8,128)(2,1)}, s32[]{:T(128)}, ...), branch_computations={%region_16.16_spmd, %region_17.17_spmd} | conditional | flops 8202487808 | bytes 317826112 | solution.py:241
  1280.7 129.1 %conditional.7 = ((f32[4,1024,12,64]{1,3,2,0:T(8,128)}, f32[2,4,2048,768]{2,3,1,0:T(8,128)})) conditional(s32[]{:T(128)} %convert_element_type.400, (f32[4,1024]{1,0:T(4,128)S(1)}, f32[4,256]{1,0:T(4,128)}, s32[]{:T(128)}, s32[256]{0:T(256)}, s32[]{:T(128)}, /*index=5*/bf16[4,2048,768]{1,2,0:T(8,128)(2,1)}, s32[]{:T(128)}, ...), branch_computations={%region_16.16_spmd, %region_17.17_spmd} | conditional | flops 8202487808 | bytes 317826112 | solution.py:241
  1414.0 129.1 %conditional.7 = ((f32[4,1024,12,64]{1,3,2,0:T(8,128)}, f32[2,4,2048,768]{2,3,1,0:T(8,128)})) conditional(s32[]{:T(128)} %convert_element_type.400, (f32[4,1024]{1,0:T(4,128)S(1)}, f32[4,256]{1,0:T(4,128)}, s32[]{:T(128)}, s32[256]{0:T(256)}, s32[]{:T(128)}, /*index=5*/bf16[4,2048,768]{1,2,0:T(8,128)(2,1)}, s32[]{:T(128)}, ...), branch_computations={%region_16.16_spmd, %region_17.17_spmd} | conditional | flops 8202487808 | bytes 317826112 | solution.py:241
  1560.4 37.8 %copy.67 = bf16[2,4,2048,768]{3,2,1,0:T(8,128)(2,1)} copy(f32[2,4,2048,768]{2,3,1,0:T(8,128)} %get-tuple-element.862) | data formatting | bytes 75497472 | tf_op jit(solution)/shard_map/while | solution.py:47
  1634.4 32.6 convolution_convert_fusion.2
  1695.8 1007.1 %reduce-scatter.6.cloned.1.call-done = bf16[2,4,1024,768]{3,2,1,0:T(8,128)(2,1)} async-done(((bf16[2,4,2048,768]{3,2,1,0:T(8,128)(2,1)}), bf16[2,4,1024,768]{3,2,1,0:T(8,128)(2,1)}) %reduce-scatter.6.cloned.1.call-update) | async-done | bytes 12582928 | tf_op jit(solution)/shard_map/reduce_scatter | solution.py:256
  2764.9 78.4 %reduce-scatter.14.cloned.1.call-done = bf16[192,768]{1,0:T(8,128)(2,1)} async-done(((bf16[3072,768]{1,0:T(8,128)(2,1)}), bf16[192,768]{1,0:T(8,128)(2,1)}) %reduce-scatter.14.cloned.1.call-update) | async-done | bytes 294928 | tf_op jit(solution)/shard_map/reduce_scatter | solution.py:325
  2843.3 78.8 %reduce-scatter.12.cloned.1.call-done = bf16[48,3072]{1,0:T(8,128)(2,1)} async-done(((bf16[768,3072]{1,0:T(8,128)(2,1)}), bf16[48,3072]{1,0:T(8,128)(2,1)}) %reduce-scatter.12.cloned.1.call-update) | async-done | bytes 294928 | tf_op jit(solution)/shard_map/reduce_scatter | solution.py:319
  2922.1 71.4 %reduce-scatter.8.cloned.1.call-done = bf16[48,2304]{1,0:T(8,128)(2,1)} async-done(((bf16[768,2304]{1,0:T(8,128)(2,1)}), bf16[48,2304]{1,0:T(8,128)(2,1)}) %reduce-scatter.8.cloned.1.call-update) | async-done | bytes 221200 | tf_op jit(solution)/shard_map/reduce_scatter | solution.py:301
  2993.7 38.4 %all-reduce.22.cloned.1.call-done = (bf16[48,2304]{1,0:T(8,128)(2,1)}, bf16[48,768]{1,0:T(8,128)(2,1)}, bf16[48,3072]{1,0:T(8,128)(2,1)}, bf16[192,768]{1,0:T(8,128)(2,1)}) async-done(((bf16[48,2304]{1,0:T(8,128)(2,1)}, bf16[48,768]{1,0:T(8,128)(2,1)}, bf16[48,3072]{1,0:T(8,128)(2,1)}, bf16[192,768]{1,0:T(8,128)(2,1)}), (bf16[48,2304]{1,0:T(8,128)(2,1)}, bf16[48,768]{1,0:T(8,128)(2,1)}, ...) | async-done | bytes 884752 | tf_op jit(solution)/shard_map/psum | solution.py:335
  3107.9 62.1 %all-reduce.17 = (bf16[768]{0:T(1024)(128)(2,1)}, bf16[768]{0:T(1024)(128)(2,1)}, bf16[1536]{0:T(1024)(128)(2,1)}, bf16[768]{0:T(1024)(128)(2,1)}, bf16[768]{0:T...) all-reduce(bf16[768]{0:T(1024)(128)(2,1)} %get-tuple-element.1012, ...), channel_id=3, replica_groups=mesh['rows'=16,'seq'=2] {'rows'}, use_global_device_ids=true, to_apply=%region_23.24.clone | all-reduce | flops 9216 | bytes 36864
  3201.7 58.4 %all-reduce.16 = (bf16[768]{0:T(1024)(128)(2,1)}, bf16[768]{0:T(1024)(128)(2,1)}, bf16[1536]{0:T(1024)(128)(2,1)}, bf16[768]{0:T(1024)(128)(2,1)}, bf16[768]{0:T...) all-reduce(bf16[768]{0:T(1024)(128)(2,1)} %dynamic-update-slice, ...), channel_id=1, replica_groups=mesh['rows'=16,'seq'=2] {'rows'}, use_global_device_ids=true, to_apply=%add | all-reduce | flops 9216 | bytes 36864
  (395 shorter events, 1445.7 us)
Async XLA Ops:
  7.2 206.6 %all-gather.7.cloned.1.call-start = ((), (), s32[]{:S(2)}) async-start(), calls=%async_computation.5 | async-start | bytes 18874368 | tf_op jit(solution)/shard_map/all_gather | solution.py:145
  58.3 310.2 %all-gather.9.cloned.1.call-start = ((), (), s32[]{:S(2)}) async-start(), calls=%async_computation.6 | async-start | bytes 18874368 | tf_op jit(solution)/shard_map/all_gather | solution.py:146
  82.6 2620.3 %reduce-scatter.6.cloned.1.call-start = ((), (), s32[]{:S(2)}) async-start(), calls=%async_computation.7 | async-start | bytes 37748736 | tf_op jit(solution)/shard_map/reduce_scatter | solution.py:256
  430.5 27.5 copy-start.6
  430.5 27.5 copy-start.7
  513.7 27.5 copy-start.6
  513.7 27.5 copy-start.7
  597.0 27.5 copy-start.6
  597.0 27.5 copy-start.7
  769.9 136.0 %copy-start.18 = (f32[4096]{0:T(1024)}, f32[4096]{0:T(1024)S(1)}, u32[]{:S(2)}) copy-start(f32[4096]{0:T(1024)S(1)} %broadcast_multiply_fusion) | copy-start | bytes 49156
  873.7 32.2 copy-start.21
  873.7 32.2 copy-start.26
  873.7 32.2 copy-start.31
  1598.2 1166.7 %reduce-scatter.10.cloned.1.call-start = ((), (), s32[]{:S(2)}) async-start(), calls=%async_computation.10 | async-start | bytes 1253376 | tf_op jit(solution)/shard_map/reduce_scatter | solution.py:307
  1608.0 1235.3 %reduce-scatter.14.cloned.1.call-start = ((), (), s32[]{:S(2)}) async-start(), calls=%async_computation.14 | async-start | bytes 5013504 | tf_op jit(solution)/shard_map/reduce_scatter | solution.py:325
  1634.3 1287.8 %reduce-scatter.12.cloned.1.call-start = ((), (), s32[]{:S(2)}) async-start(), calls=%async_computation.12 | async-start | bytes 5013504 | tf_op jit(solution)/shard_map/reduce_scatter | solution.py:319
  1667.0 1326.6 %reduce-scatter.8.cloned.1.call-start = ((), (), s32[]{:S(2)}) async-start(), calls=%async_computation.8 | async-start | bytes 3760128 | tf_op jit(solution)/shard_map/reduce_scatter | solution.py:301
  2732.4 301.2 %copy-start.32 = (u32[32]{0:T(128)S(1)}, u32[32]{0:T(128)}, u32[]{:S(2)}) copy-start(u32[32]{0:T(128)} %constant.242) | copy-start | bytes 388
  2754.8 277.3 %all-reduce.22.cloned.1.call-start = ((), (), s32[]{:S(2)}) async-start(), calls=%async_computation.16 | async-start | bytes 1769472 | tf_op jit(solution)/shard_map/psum | solution.py:335
  2993.6 295.6 %all-gather.13.cloned.1.call-start = ((), (), s32[]{:S(2)}) async-start(), calls=%async_computation.11 | async-start | bytes 1253376 | tf_op jit(solution)/shard_map/all_gather | solution.py:359
  3032.1 260.0 %all-gather.11.cloned.1.call-start = ((), (), s32[]{:S(2)}) async-start(), calls=%async_computation.9 | async-start | bytes 3760128 | tf_op jit(solution)/shard_map/all_gather | solution.py:353
  3032.7 264.9 %all-gather.17.cloned.1.call-start = ((), (), s32[]{:S(2)}) async-start(), calls=%async_computation.15 | async-start | bytes 5013504 | tf_op jit(solution)/shard_map/all_gather | solution.py:377
  3033.5 271.0 %all-gather.15.cloned.1.call-start = ((), (), s32[]{:S(2)}) async-start(), calls=%async_computation.13 | async-start | bytes 5013504 | tf_op jit(solution)/shard_map/all_gather | solution.py:371
  3042.7 30.7 copy-start.15
  (41 other events, 465.4 us)
Sparse Core Ops, SparseCore 0:
  58.4 155.3 all-gather.6
  215.9 152.5 all-gather.8
  1598.3 1104.5 reduce-scatter.5
  2707.0 57.9 reduce-scatter.9
  2768.6 74.6 reduce-scatter.13
  2847.5 74.5 reduce-scatter.11
  2926.6 66.9 reduce-scatter.7
  2996.1 35.9 all-reduce.21
  3034.4 38.3 all-gather.12
  3074.9 46.2 all-gather.10
  3123.5 52.6 all-gather.16
  3178.3 52.2 all-gather.14
where the time goes:
time: 3330 us; the launch traced here: 3320 us
  waiting for transfers between devices  1530 us (46%)
  matrix products  942 us (28%)
  other arithmetic  376 us (11%)
  local copies, waits for them, and re-layouts  299 us (9%)
  blocking collectives  132 us (4%)
    reduce_scatter x1, waiting for transfers between devices, local(): lax.psum_scatter(grad_full.astype(jnp.bfloat16), 'seq', scatter_dimension...  1010 us
    all_gather x1, waiting for transfers between devices, local(): lax.all_gather(value_rows, 'seq', axis=1, tiled=True)  155 us
    dot_general x4, matrix products, back_update(): jnp.einsum('rqhd,rkhd->rhqk', grad_attended, value_heads, preferred_eleme...  123 us
    unnamed x2, blocking collectives  121 us
    dot_general x4, matrix products, attend_update(): jnp.einsum('rhqk,rkhd->rqhd', prob_block.astype(jnp.bfloat16), split_head...  110 us
    dot_general x4, matrix products, back_update(): jnp.einsum('rqhd,rkhd->rhqk', queries, key_heads, preferred_element_type=...  89.5 us
    all_gather x1, waiting for transfers between devices, local(): lax.all_gather(key_rows, 'seq', axis=1, tiled=True)  88.6 us
    dot_general x4, matrix products, back_update(): jnp.einsum('rhqk,rqhd->rkhd', prob_block.astype(jnp.bfloat16), grad_atten...  87.8 us
  transfers between devices with their start and end apart: 12, of which 8 were waited for; matrix products, arithmetic and copies ran while one was open for 11% of the time, Pallas kernels for 0%

commit v1 on v0

--- a/solution.py
+++ b/solution.py
@@ -3,6 +3,8 @@
 import jax
 import jax.numpy as jnp
 from jax import lax
+from jax.experimental import pallas as pl
+from jax.experimental.pallas import tpu as pltpu
 from jax.sharding import PartitionSpec as P
 
 HEADS = 12
@@ -384,38 +386,558 @@
     return (layer_output, input_grad) + tuple(totals)
 
 
+MIB = 1 << 20
+LOG2E = 1.4426950408889634
+GELU_C = 0.7978845608028654
+GELU_A = 0.044715
+BLOCK = 256
+f32 = jnp.float32
+bf16 = jnp.bfloat16
+
+
+def dot_nn(a, b):
+    return lax.dot_general(a, b, (((1,), (0,)), ((), ())), preferred_element_type=f32)
+
+
+def dot_nt(a, b):
+    return lax.dot_general(a, b, (((1,), (1,)), ((), ())), preferred_element_type=f32)
+
+
+def norm_parts(values):
+    center = values - jnp.mean(values, axis=-1, keepdims=True)
+    variance = jnp.mean(center * center, axis=-1, keepdims=True)
+    inverse = lax.rsqrt(variance + EPSILON)
+    return center * inverse, inverse
+
+
+def row_sums(values):
+    rows, cols = values.shape
+    return jnp.sum(values.reshape(rows // 8, 8, cols), axis=0)
+
+
+def whole(shape):
+    return pl.BlockSpec(shape, lambda *_: (0,) * len(shape), pipeline_mode=pl.Buffered(1))
+
+
+def call(kernel, name, grid, in_specs, out_specs, out_shape, scratch, flops, moved, vmem, prefetch=0):
+    return pl.pallas_call(
+        kernel,
+        out_shape=out_shape,
+        grid_spec=pltpu.PrefetchScalarGridSpec(
+            num_scalar_prefetch=prefetch,
+            grid=grid,
+            in_specs=in_specs,
+            out_specs=out_specs,
+            scratch_shapes=scratch,
+        ),
+        compiler_params=pltpu.CompilerParams(vmem_limit_bytes=vmem * MIB),
+        cost_estimate=pl.CostEstimate(flops=flops, bytes_accessed=moved, transcendentals=0),
+        name=name,
+    )
+
+
+def qkv_kernel(x_ref, gain_ref, shift_ref, w_ref, bias_ref, q_ref, k_ref, v_ref, kt_ref, vt_ref):
+    width = x_ref.shape[1]
+    hat, _ = norm_parts(x_ref[...].astype(f32))
+    normed = (hat * gain_ref[...] + shift_ref[...]).astype(bf16)
+    q_ref[...] = (dot_nn(normed, w_ref[:, :width]) + bias_ref[:, :width]).astype(bf16)
+    keys = dot_nn(normed, w_ref[:, width : 2 * width])
+    k_ref[...] = keys.astype(bf16)
+    kt_ref[...] = jnp.transpose(keys).astype(bf16)
+    values = dot_nn(normed, w_ref[:, 2 * width :]) + bias_ref[:, width:]
+    v_ref[...] = values.astype(bf16)
+    vt_ref[...] = jnp.transpose(values).astype(bf16)
+
+
+def project_qkv(x, gain, shift, weight, bias):
+    tokens, width = x.shape
+    tile = 512
+    flat = pl.BlockSpec((tile, width), lambda t: (t, 0))
+    turned = pl.BlockSpec((width, tile), lambda t: (0, t))
+    return call(
+        qkv_kernel,
+        "qkv_forward",
+        (tokens // tile,),
+        [flat, whole((1, width)), whole((1, width)), whole(weight.shape), whole((1, 2 * width))],
+        [flat, flat, flat, turned, turned],
+        [jax.ShapeDtypeStruct((tokens, width), bf16)] * 3
+        + [jax.ShapeDtypeStruct((width, tokens), bf16)] * 2,
+        [],
+        2 * tokens * width * 3 * width,
+        tokens * width * 12 + weight.size * 2,
+        60,
+    )(x, gain[None], shift[None], weight, bias[None])
+
+
+def attend_kernel(low_ref, start_ref, q_ref, k_ref, vt_ref, att_ref, lse_ref):
+    row = pl.program_id(0)
+    length = q_ref.shape[0]
+    blocks = length // BLOCK
+    scale = HEAD_DIM**-0.5 * LOG2E
+    lanes = lax.broadcasted_iota(jnp.int32, (BLOCK, 2 * HEAD_DIM), 1)
+    slots = lax.broadcasted_iota(jnp.int32, (BLOCK, BLOCK), 0)
+    query_iota = lax.broadcasted_iota(jnp.int32, (BLOCK, BLOCK), 1)
+
+    def query_block(qb, _):
+        q_at = pl.ds(pl.multiple_of(qb * BLOCK, BLOCK), BLOCK)
+        queries = q_ref[q_at, :]
+        heads = [
+            jnp.where(lanes < HEAD_DIM, queries, jnp.zeros_like(queries)),
+            jnp.where(lanes >= HEAD_DIM, queries, jnp.zeros_like(queries)),
+        ]
+        start = start_ref[0, :, q_at]
+
+        def scored(kb, extra):
+            k_at = pl.ds(pl.multiple_of(kb * BLOCK, BLOCK), BLOCK)
+            keys = k_ref[k_at, :]
+            allowed = slots >= start - kb * BLOCK
+            if extra is not None:
+                allowed = allowed & extra
+            return k_at, [
+                jnp.where(allowed, dot_nt(keys, heads[h]) * scale, NEGATIVE) for h in range(2)
+            ]
+
+        k_at, scores = scored(qb, slots <= query_iota)
+        state = []
+        for h in range(2):
+            top = jnp.max(scores[h], axis=0, keepdims=True)
+            probs = jnp.exp2(scores[h] - top)
+            total = jnp.sum(probs, axis=0, keepdims=True)
+            out = dot_nn(vt_ref[pl.ds(h * HEAD_DIM, HEAD_DIM), k_at], probs.astype(bf16))
+            state += [top, total, out]
+
+        def key_block(kb, state):
+            k_at, scores = scored(kb, None)
+            fresh = []
+            for h in range(2):
+                top, total, out = state[3 * h : 3 * h + 3]
+                new_top = jnp.maximum(top, jnp.max(scores[h], axis=0, keepdims=True))
+                probs = jnp.exp2(scores[h] - new_top)
+                factor = jnp.exp2(top - new_top)
+                total = total * factor + jnp.sum(probs, axis=0, keepdims=True)
+                out = out * factor + dot_nn(
+                    vt_ref[pl.ds(h * HEAD_DIM, HEAD_DIM), k_at], probs.astype(bf16)
+                )
+                fresh += [new_top, total, out]
+            return tuple(fresh)
+
+        state = lax.fori_loop(low_ref[row * blocks + qb], qb, key_block, tuple(state))
+        outs = []
+        for h in range(2):
+            top, total, out = state[3 * h : 3 * h + 3]
+            outs.append(out / total)
+            lse_ref[0, h : h + 1, q_at] = top + jnp.log2(total)
+        att_ref[q_at, :] = jnp.transpose(jnp.concatenate(outs, axis=0)).astype(bf16)
+        return 0
+
+    lax.fori_loop(0, blocks, query_block, 0)
+
+
+def attend(low, start, q, k, vt, rows):
+    tokens, width = q.shape
+    length = tokens // rows
+    pairs = width // (2 * HEAD_DIM)
+    flat = pl.BlockSpec((length, 2 * HEAD_DIM), lambda r, p, *_: (r, p))
+    turned = pl.BlockSpec((2 * HEAD_DIM, length), lambda r, p, *_: (p, r))
+    return call(
+        attend_kernel,
+        "attention_forward",
+        (rows, pairs),
+        [pl.BlockSpec((1, 1, length), lambda r, p, *_: (r, 0, 0)), flat, flat, turned],
+        [flat, pl.BlockSpec((1, 2, length), lambda r, p, *_: (p, 0, r))],
+        [
+            jax.ShapeDtypeStruct((tokens, width), bf16),
+            jax.ShapeDtypeStruct((pairs, 2, tokens), f32),
+        ],
+        [],
+        2 * tokens * length * width,
+        tokens * width * 8,
+        60,
+        prefetch=1,
+    )(low, start, q, k, vt)
+
+
+def attend_back_kernel(
+    high_ref, start_ref, q_ref, k_ref, kt_ref, v_ref, do_ref, lse_ref, delta_ref,
+    dq_ref, dk_ref, dv_ref, q0, q1, do0, do1, dqt,
+):
+    row = pl.program_id(0)
+    length = q_ref.shape[0]
+    blocks = length // BLOCK
+    scale = HEAD_DIM**-0.5 * LOG2E
+    lanes = lax.broadcasted_iota(jnp.int32, (length, 2 * HEAD_DIM), 1)
+    zero = jnp.zeros((length, 2 * HEAD_DIM), bf16)
+    queries = q_ref[...]
+    q0[...] = jnp.where(lanes < HEAD_DIM, queries, zero)
+    q1[...] = jnp.where(lanes >= HEAD_DIM, queries, zero)
+    grads = do_ref[...]
+    do0[...] = jnp.where(lanes < HEAD_DIM, grads, zero)
+    do1[...] = jnp.where(lanes >= HEAD_DIM, grads, zero)
+    dqt[...] = jnp.zeros_like(dqt)
+    slots = lax.broadcasted_iota(jnp.int32, (BLOCK, BLOCK), 0)
+    query_iota = lax.broadcasted_iota(jnp.int32, (BLOCK, BLOCK), 1)
+
+    def key_block(kb, _):
+        k_at = pl.ds(pl.multiple_of(kb * BLOCK, BLOCK), BLOCK)
+        keys = k_ref[k_at, :]
+        values = v_ref[k_at, :]
+
+        def visit(qb, extra):
+            q_at = pl.ds(pl.multiple_of(qb * BLOCK, BLOCK), BLOCK)
+            allowed = slots >= start_ref[0, :, q_at] - kb * BLOCK
+            if extra is not None:
+                allowed = allowed & extra
+            dk = dv = None
+            for h, (qh, doh) in enumerate(((q0, do0), (q1, do1))):
+                q_head = qh[q_at, :]
+                do_head = doh[q_at, :]
+                scores = dot_nt(keys, q_head) * scale
+                probs = jnp.where(allowed, jnp.exp2(scores - lse_ref[0, h : h + 1, q_at]), 0.0)
+                grad_probs = dot_nt(values, do_head)
+                grad_scores = (probs * (grad_probs - delta_ref[0, h : h + 1, q_at])).astype(bf16)
+                dv_part = dot_nn(probs.astype(bf16), do_head)
+                dk_part = dot_nn(grad_scores, q_head)
+                dk = dk_part if dk is None else dk + dk_part
+                dv = dv_part if dv is None else dv + dv_part
+                at = pl.ds(h * HEAD_DIM, HEAD_DIM)
+                dqt[at, q_at] += dot_nn(kt_ref[at, k_at], grad_scores)
+            return dk, dv
+
+        def query_block(qb, state):
+            dk, dv = visit(qb, None)
+            return state[0] + dk, state[1] + dv
+
+        dk, dv = lax.fori_loop(
+            kb + 1, high_ref[row * blocks + kb] + 1, query_block, visit(kb, slots <= query_iota)
+        )
+        dk_ref[k_at, :] = (dk * HEAD_DIM**-0.5).astype(bf16)
+        dv_ref[k_at, :] = dv.astype(bf16)
+        return 0
+
+    lax.fori_loop(0, blocks, key_block, 0)
+
+    def turn(qb, _):
+        q_at = pl.ds(pl.multiple_of(qb * BLOCK, BLOCK), BLOCK)
+        dq_ref[q_at, :] = (jnp.transpose(dqt[:, q_at]) * HEAD_DIM**-0.5).astype(bf16)
+        return 0
+
+    lax.fori_loop(0, blocks, turn, 0)
+
+
+def attend_back(high, start, q, k, kt, v, do, lse, delta, rows):
+    tokens, width = q.shape
+    length = tokens // rows
+    pairs = width // (2 * HEAD_DIM)
+    flat = pl.BlockSpec((length, 2 * HEAD_DIM), lambda r, p, *_: (r, p))
+    turned = pl.BlockSpec((2 * HEAD_DIM, length), lambda r, p, *_: (p, r))
+    lined = pl.BlockSpec((1, 2, length), lambda r, p, *_: (p, 0, r))
+    return call(
+        attend_back_kernel,
+        "attention_backward",
+        (rows, pairs),
+        [pl.BlockSpec((1, 1, length), lambda r, p, *_: (r, 0, 0)), flat, flat, turned, flat, flat, lined, lined],
+        [flat, flat, flat],
+        [jax.ShapeDtypeStruct((tokens, width), bf16)] * 3,
+        [pltpu.VMEM((length, 2 * HEAD_DIM), bf16)] * 4 + [pltpu.VMEM((2 * HEAD_DIM, length), f32)],
+        5 * tokens * length * width,
+        tokens * width * 16,
+        60,
+        prefetch=1,
+    )(high, start, q, k, kt, v, do, lse, delta)
+
+
+def mlp_kernel(
+    x_ref, att_ref, cot_ref, proj_ref, projb_ref, gain_ref, shift_ref, fc_ref, fcb_ref, out_ref, outb_ref,
+    pick_ref,
+    y_ref, gm_ref, do_ref, delta_ref, dfc_ref, doutt_ref, dproj_ref, small_ref, dfcb_ref,
+    dfc, doutt, dproj, sums, dfcb, stage, sem,
+):
+    step = pl.program_id(0)
+    steps = pl.num_programs(0)
+    tile, width = x_ref.shape
+    hidden = fc_ref.shape[1]
+    chunk = 768
+
+    @pl.when(step == 0)
+    def _():
+        dfc[...] = jnp.zeros_like(dfc)
+        doutt[...] = jnp.zeros_like(doutt)
+        dproj[...] = jnp.zeros_like(dproj)
+        sums[...] = jnp.zeros_like(sums)
+        dfcb[...] = jnp.zeros_like(dfcb)
+
+    att = att_ref[...]
+    middle = x_ref[...].astype(f32) + BRANCH * (dot_nn(att, proj_ref[...]) + projb_ref[...])
+    hat, inverse = norm_parts(middle)
+    normed_f = hat * gain_ref[...] + shift_ref[...]
+    normed = normed_f.astype(bf16)
+    normed_t = jnp.transpose(normed_f).astype(bf16)
+    cot = cot_ref[...].astype(f32)
+    grad_two = (BRANCH * cot).astype(bf16)
+    grad_two_f = grad_two.astype(f32)
+    grad_two_t = jnp.transpose(grad_two_f).astype(bf16)
+    branch = jnp.zeros((tile, width), f32)
+    grad_normed = jnp.zeros((tile, width), f32)
+    for at in range(0, hidden, chunk):
+        cols = pl.ds(at, chunk)
+        pre = dot_nn(normed, fc_ref[:, cols]) + fcb_ref[:, cols]
+        square = pre * pre
+        half = 0.5 + 0.5 * jnp.tanh(pre * (GELU_C + GELU_C * GELU_A * square))
+        act = pre * half
+        slope = half + act * (1.0 - half) * (2.0 * GELU_C + 6.0 * GELU_C * GELU_A * square)
+        act = act.astype(bf16)
+        grad_pre_f = dot_nt(grad_two, out_ref[cols, :]) * slope
+        grad_pre = grad_pre_f.astype(bf16)
+        branch += dot_nn(act, out_ref[cols, :])
+        grad_normed += dot_nt(grad_pre, fc_ref[:, cols])
+        dfc[:, cols] += dot_nn(normed_t, grad_pre)
+        doutt[:, cols] += dot_nn(grad_two_t, act)
+        dfcb[:, cols] += row_sums(grad_pre.astype(f32))
+    y_ref[...] = (middle + BRANCH * (branch + outb_ref[...])).astype(bf16)
+    scaled = grad_normed * gain_ref[...]
+    mean_one = jnp.mean(scaled, axis=-1, keepdims=True)
+    mean_two = jnp.mean(scaled * hat, axis=-1, keepdims=True)
+    grad_middle = cot + inverse * (scaled - mean_one - hat * mean_two)
+    gm_ref[...] = grad_middle
+    grad_one_f = BRANCH * grad_middle
+    grad_one = grad_one_f.astype(bf16)
+    grad_att = dot_nt(grad_one, proj_ref[...]).astype(bf16)
+    do_ref[...] = grad_att
+    dproj[...] += dot_nn(jnp.transpose(att.astype(f32)).astype(bf16), grad_one)
+    product = grad_att.astype(f32) * att.astype(f32)
+    upper = product.astype(bf16)
+    lower = (product - upper.astype(f32)).astype(bf16)
+    delta = dot_nt(pick_ref[...], upper) + dot_nt(pick_ref[...], lower)
+    for pair in range(delta_ref.shape[0]):
+        delta_ref[pair] = delta[2 * pair : 2 * pair + 2, :]
+    sums[0:8, :] += row_sums(grad_normed * hat)
+    sums[8:16, :] += row_sums(grad_normed)
+    sums[16:24, :] += row_sums(grad_two_f)
+    sums[24:32, :] += row_sums(grad_one.astype(f32))
+
+    @pl.when(step == steps - 1)
+    def _():
+        for source, target in ((dfc, dfc_ref), (doutt, doutt_ref)):
+            stage[...] = source[...].astype(bf16)
+            copy = pltpu.make_async_copy(stage, target, sem)
+            copy.start()
+            copy.wait()
+        dproj_ref[...] = dproj[...].astype(bf16)
+        small_ref[...] = sums[...]
+        dfcb_ref[...] = dfcb[...]
+
+
+def feed_forward(x, att, cot, proj_weight, proj_bias, gain, shift, fc_weight, fc_bias, out_weight, out_bias):
+    tokens, width = x.shape
+    hidden = fc_weight.shape[1]
+    heads = width // HEAD_DIM
+    tile = 256
+    pick = (jnp.arange(16)[:, None] == jnp.arange(width)[None, :] // HEAD_DIM).astype(bf16)
+    flat = pl.BlockSpec((tile, width), lambda t: (t, 0))
+    return call(
+        mlp_kernel,
+        "feed_forward",
+        (tokens // tile,),
+        [flat, flat, flat, whole((width, width)), whole((1, width)), whole((1, width)), whole((1, width)),
+         whole(fc_weight.shape), whole((1, hidden)), whole(out_weight.shape), whole((1, width)), whole((16, width))],
+        [flat, flat, flat, pl.BlockSpec((heads // 2, 2, tile), lambda t: (0, 0, t)),
+         pl.BlockSpec(memory_space=pl.ANY), pl.BlockSpec(memory_space=pl.ANY),
+         whole((width, width)), whole((32, width)), whole((8, hidden))],
+        [
+            jax.ShapeDtypeStruct((tokens, width), bf16),
+            jax.ShapeDtypeStruct((tokens, width), f32),
+            jax.ShapeDtypeStruct((tokens, width), bf16),
+            jax.ShapeDtypeStruct((heads // 2, 2, tokens), f32),
+            jax.ShapeDtypeStruct((width, hidden), bf16),
+            jax.ShapeDtypeStruct((width, hidden), bf16),
+            jax.ShapeDtypeStruct((width, width), bf16),
+            jax.ShapeDtypeStruct((32, width), f32),
+            jax.ShapeDtypeStruct((8, hidden), f32),
+        ],
+        [
+            pltpu.VMEM((width, hidden), f32),
+            pltpu.VMEM((width, hidden), f32),
+            pltpu.VMEM((width, width), f32),
+            pltpu.VMEM((32, width), f32),
+            pltpu.VMEM((8, hidden), f32),
+            pltpu.VMEM((width, hidden), bf16),
+            pltpu.SemaphoreType.DMA,
+        ],
+        2 * tokens * width * (3 * width + 6 * hidden),
+        tokens * width * 14,
+        62,
+    )(x, att, cot, proj_weight, proj_bias[None], gain[None], shift[None], fc_weight, fc_bias[None],
+      out_weight, out_bias[None], pick)
+
+
+def qkv_weight_kernel(x_ref, gain_ref, shift_ref, dq_ref, dk_ref, dv_ref, dw_ref, small_ref, acc, sums):
+    step = pl.program_id(0)
+    width = x_ref.shape[1]
+
+    @pl.when(step == 0)
+    def _():
+        acc[...] = jnp.zeros_like(acc)
+        sums[...] = jnp.zeros_like(sums)
+
+    hat, _ = norm_parts(x_ref[...].astype(f32))
+    normed_t = jnp.transpose(hat * gain_ref[...] + shift_ref[...]).astype(bf16)
+    for i, ref in enumerate((dq_ref, dk_ref, dv_ref)):
+        acc[:, i * width : (i + 1) * width] += dot_nn(normed_t, ref[...])
+    sums[0:8, :] += row_sums(dq_ref[...].astype(f32))
+    sums[8:16, :] += row_sums(dv_ref[...].astype(f32))
+
+    @pl.when(step == pl.num_programs(0) - 1)
+    def _():
+        dw_ref[...] = acc[...].astype(bf16)
+        small_ref[...] = sums[...]
+
+
+def qkv_weight_back(x, gain, shift, dq, dk, dv):
+    tokens, width = x.shape
+    tile = 512
+    flat = pl.BlockSpec((tile, width), lambda t: (t, 0))
+    return call(
+        qkv_weight_kernel,
+        "qkv_weight_gradient",
+        (tokens // tile,),
+        [flat, whole((1, width)), whole((1, width)), flat, flat, flat],
+        [whole((width, 3 * width)), whole((16, width))],
+        [jax.ShapeDtypeStruct((width, 3 * width), bf16), jax.ShapeDtypeStruct((16, width), f32)],
+        [pltpu.VMEM((width, 3 * width), f32), pltpu.VMEM((16, width), f32)],
+        2 * tokens * width * 3 * width,
+        tokens * width * 8,
+        60,
+    )(x, gain[None], shift[None], dq, dk, dv)
+
+
+def qkv_input_kernel(x_ref, gain_ref, w_ref, dq_ref, dk_ref, dv_ref, gm_ref, dx_ref, small_ref, sums):
+    step = pl.program_id(0)
+    width = x_ref.shape[1]
+
+    @pl.when(step == 0)
+    def _():
+        sums[...] = jnp.zeros_like(sums)
+
+    hat, inverse = norm_parts(x_ref[...].astype(f32))
+    grad_normed = (
+        dot_nt(dq_ref[...], w_ref[:, :width])
+        + dot_nt(dk_ref[...], w_ref[:, width : 2 * width])
+        + dot_nt(dv_ref[...], w_ref[:, 2 * width :])
+    )
+    scaled = grad_normed * gain_ref[...]
+    mean_one = jnp.mean(scaled, axis=-1, keepdims=True)
+    mean_two = jnp.mean(scaled * hat, axis=-1, keepdims=True)
+    dx_ref[...] = gm_ref[...] + inverse * (scaled - mean_one - hat * mean_two)
+    sums[0:8, :] += row_sums(grad_normed * hat)
+    sums[8:16, :] += row_sums(grad_normed)
+
+    @pl.when(step == pl.num_programs(0) - 1)
+    def _():
+        small_ref[...] = sums[...]
+
+
+def qkv_input_back(x, gain, weight, dq, dk, dv, grad_middle):
+    tokens, width = x.shape
+    tile = 512
+    flat = pl.BlockSpec((tile, width), lambda t: (t, 0))
+    return call(
+        qkv_input_kernel,
+        "qkv_input_gradient",
+        (tokens // tile,),
+        [flat, whole((1, width)), whole(weight.shape), flat, flat, flat, flat],
+        [flat, whole((16, width))],
+        [jax.ShapeDtypeStruct((tokens, width), f32), jax.ShapeDtypeStruct((16, width), f32)],
+        [pltpu.VMEM((16, width), f32)],
+        2 * tokens * width * 3 * width,
+        tokens * width * 16,
+        60,
+    )(x, gain[None], weight, dq, dk, dv, grad_middle)
+
+
+def to_rows(mine):
+    me = lax.axis_index("seq")
+    half = mine.shape[0] // 2
+    kept = lax.dynamic_slice_in_dim(mine, me * half, half, 0)
+    sent = lax.dynamic_slice_in_dim(mine, (1 - me) * half, half, 0)
+    got = lax.ppermute(sent, "seq", [(0, 1), (1, 0)])
+    first = jnp.where(me == 0, kept, got)
+    second = jnp.where(me == 0, got, kept)
+    return jnp.concatenate((first, second), axis=1)
+
+
+def from_rows(rows, dtype):
+    me = lax.axis_index("seq")
+    length = rows.shape[1] // 2
+    kept = lax.dynamic_slice_in_dim(rows, me * length, length, 1)
+    sent = lax.dynamic_slice_in_dim(rows, (1 - me) * length, length, 1).astype(bf16)
+    got = lax.ppermute(sent, "seq", [(0, 1), (1, 0)]).astype(dtype)
+    return jnp.concatenate((jnp.where(me == 0, kept, got), jnp.where(me == 0, got, kept)), axis=0)
+
+
+def row_local(
+    block_input, segment_ids, norm1_gain, norm1_shift, qkv_weight, qv_bias, proj_weight, proj_bias,
+    norm2_gain, norm2_shift, fc_weight, fc_bias, out_weight, out_bias, out_cotangent,
+):
+    width = block_input.shape[-1]
+    segments = to_rows(segment_ids)
+    x = to_rows(block_input)
+    rows, length, _ = x.shape
+    tokens = rows * length
+    cot = to_rows(out_cotangent)
+    slot = jnp.arange(length, dtype=jnp.int32)[None]
+    ends = [jnp.sum((segments <= doc).astype(jnp.int32), axis=1, keepdims=True) for doc in range(2)]
+    start = jnp.where(
+        segments == 0, 0, jnp.where(segments == 1, ends[0], jnp.where(segments == 2, ends[1], slot))
+    )
+    low_block = start[:, ::BLOCK] // BLOCK
+    blocks = length // BLOCK
+    high_block = jnp.sum(
+        (low_block[:, None, :] <= jnp.arange(blocks)[None, :, None]).astype(jnp.int32), axis=2
+    ) - 1
+    start = start[:, None, :]
+    low_block = low_block.reshape(-1)
+    high_block = high_block.reshape(-1)
+    x = x.reshape(tokens, width)
+    cot = cot.reshape(tokens, width)
+    q, k, v, kt, vt = project_qkv(x, norm1_gain, norm1_shift, qkv_weight, qv_bias)
+    att, lse = attend(low_block, start, q, k, vt, rows)
+    y, grad_middle, grad_att, delta, dfc, doutt, dproj, small_two, dfcb = feed_forward(
+        x, att, cot, proj_weight, proj_bias, norm2_gain, norm2_shift, fc_weight, fc_bias, out_weight, out_bias
+    )
+    both = ("rows", "seq")
+    dfc, doutt, dproj = lax.psum((dfc, doutt, dproj), both)
+    layer_output = from_rows(y.reshape(rows, length, width), bf16)
+    dq, dk, dv = attend_back(high_block, start, q, k, kt, v, grad_att, lse, delta, rows)
+    dqkv, small_qv = qkv_weight_back(x, norm1_gain, norm1_shift, dq, dk, dv)
+    dqkv = lax.psum(dqkv, both)
+    dx, small_one = qkv_input_back(x, norm1_gain, qkv_weight, dq, dk, dv, grad_middle)
+    input_grad = from_rows(dx.reshape(rows, length, width), f32)
+    small = jnp.concatenate((small_two, small_qv, small_one), axis=0)
+    small = jnp.sum(small.reshape(-1, 8, width), axis=1)
+    small = jnp.concatenate((small.reshape(-1), jnp.sum(dfcb, axis=0)))
+    small = lax.psum(small, both)
+    line = lambda i, n=1: small[i * width : (i + n) * width]
+    return (
+        layer_output,
+        input_grad,
+        line(6),
+        line(7),
+        dqkv.astype(f32),
+        line(4, 2),
+        dproj.astype(f32),
+        line(3),
+        line(0),
+        line(1),
+        dfc.astype(f32),
+        small[8 * width :],
+        jnp.transpose(doutt).astype(f32),
+        line(2),
+    )
+
+
 def solution(mesh):
-    in_specs = (
-        P("rows", "seq", None),
-        P("rows", "seq"),
-        P(),
-        P(),
-        P(),
-        P(),
-        P(),
-        P(),
-        P(),
-        P(),
-        P(),
-        P(),
-        P(),
-        P(),
-        P("rows", "seq", None),
-    )
-    out_specs = (
-        P("rows", "seq", None),
-        P("rows", "seq", None),
-        P(),
-        P(),
-        P(),
-        P(),
-        P(),
-        P(),
-        P(),
-        P(),
-        P(),
-        P(),
-        P(),
-        P(),
-    )
-    return jax.shard_map(local, mesh=mesh, in_specs=in_specs, out_specs=out_specs, check_vma=False)
+    rows_spec = P("rows", "seq", None)
+    in_specs = (rows_spec, P("rows", "seq")) + (P(),) * 12 + (rows_spec,)
+    out_specs = (rows_spec, rows_spec) + (P(),) * 12
+    body = row_local if mesh.shape["seq"] == 2 else local
+    return jax.shard_map(body, mesh=mesh, in_specs=in_specs, out_specs=out_specs, check_vma=False)

time: 3330 us -> 1180 us (0.35)
  waiting for transfers between devices: 1530 us -> 209 us
  matrix products: 942 us -> 0 us
  Pallas kernels: 0 us -> 515 us
  other arithmetic: 376 us -> 53.1 us
  local copies, waits for them, and re-layouts: 299 us -> 29.8 us
  blocking collectives: 132 us -> 321 us
    reduce_scatter x5 -> x0, waiting for transfers between devices: 1250 us -> none  [the longest x1 1010 us: local(): lax.psum_scatter(grad_full.astype(jnp.bfloat16), 'seq', scatter_dimension...]
    dot_general x40 -> x0, matrix products: 942 us -> none  [the longest x4 123 us: back_update(): jnp.einsum('rqhd,rkhd->rhqk', grad_attended, value_heads, preferred_eleme...]
    pallas_call x0 -> x6, Pallas kernels: none -> 515 us  [the longest x1 173 us: feed_forward(): call(mlp_kernel, 'feed_forward', (tokens // tile,), [flat, flat, flat, wh...]
    psum x1, blocking collectives: 5.66 us -> 321 us  [row_local(): small = lax.psum(small, both)]
    all_gather x6 -> x0, waiting for transfers between devices: 243 us -> none  [the longest x1 155 us: local(): lax.all_gather(value_rows, 'seq', axis=1, tiled=True)]
    reduce_sum x13 -> x4, other arithmetic: 151 us -> 0.38 us  [the longest x1 0.16 us: row_local(): jnp.sum((segments <= doc).astype(jnp.int32), axis=1, keepdims=True)]
    ppermute x0 -> x5, waiting for transfers between devices: none -> 127 us  [the longest x3 127 us: to_rows(): got = lax.ppermute(sent, 'seq', [(0, 1), (1, 0)])]
    unnamed x2 -> x0, blocking collectives: 121 us -> none
  transfers between devices with their start and end apart: 12 -> 6, of which waited for: 8 -> 2; matrix products, arithmetic and copies ran while one was open for 11% -> 4% of each run, Pallas kernels for 0% -> 2%
where the time goes in v1:
time: 1180 us; the launch traced here: 1160 us
  Pallas kernels  515 us (44%)
  blocking collectives  321 us (27%)
  waiting for transfers between devices  209 us (18%)
  other arithmetic  53.1 us (4%)
  local copies, waits for them, and re-layouts  29.8 us (3%)
  starting transfers between devices  21.3 us (2%)
  between operations  14.3 us (1%)
    psum x1, blocking collectives, row_local(): small = lax.psum(small, both)  321 us
    pallas_call x1, Pallas kernels, feed_forward(): call(mlp_kernel, 'feed_forward', (tokens // tile,), [flat, flat, flat, wh...  173 us
    pallas_call x1, Pallas kernels, attend_back(): call(attend_back_kernel, 'attention_backward', (rows, pairs), [pl.BlockSp...  161 us
    ppermute x3, waiting for transfers between devices, to_rows(): got = lax.ppermute(sent, 'seq', [(0, 1), (1, 0)])  127 us
    pallas_call x1, Pallas kernels, attend(): call(attend_kernel, 'attention_forward', (rows, pairs), [pl.BlockSpec((1,...  104 us
    psum x1, waiting for transfers between devices, row_local(): dfc, doutt, dproj = lax.psum((dfc, doutt, dproj), both)  81.6 us
    pallas_call x1, Pallas kernels, qkv_input_back(): call(qkv_input_kernel, 'qkv_input_gradient', (tokens // tile,), [flat, wh...  27.2 us
    pallas_call x1, Pallas kernels, qkv_weight_back(): call(qkv_weight_kernel, 'qkv_weight_gradient', (tokens // tile,), [flat,...  26.7 us
  transfers between devices with their start and end apart: 6, of which 2 were waited for; matrix products, arithmetic and copies ran while one was open for 4% of the time, Pallas kernels for 2%

profile of v1, /device:TPU:0, one launch (start us, length us, event | category | flops | bytes accessed | tf_op | source)
XLA Modules:
  0.0 1163.0 jit_solution(9582167569828664985)
XLA Ops:
  7.3 3.9 constant_dynamic-slice_fusion.1
  11.2 3.0 collective-permute-start.2
  22.9 127.2 %collective-permute-done.1 = s32[2,1024]{1,0:T(2,128)S(1)} collective-permute-done((s32[2,1024]{1,0:T(2,128)S(1)}, s32[2,1024]{1,0:T(2,128)S(1)}, u32[]{:S(2)}, u32[]{:S(2)}) %collective-permute-start.1) | collective-permute-done | bytes 8224 | tf_op jit(solution)/shard_map/ppermute | solution.py:862
  154.3 5.1 broadcast_select_fusion.3
  159.4 3.0 pad_maximum_fusion.2
  162.4 3.1 pad_maximum_fusion.1
  165.5 23.4 %qkv_forward.1 = (bf16[4096,768]{1,0:T(8,128)(2,1)}, bf16[4096,768]{1,0:T(8,128)(2,1)}, bf16[4096,768]{1,0:T(8,128)(2,1)}, bf16[768,4096]{1,0:T(8,128)(2,1)}, bf16[768,4096]{1,0:T(8,128)(2,1)}) custom-call(bf16[4096,768]{1,0:T(8,128)(2,1)} %bitcast.13, f32[1,768]{1,0:T(1,128)} %broadcast_in_dim.73.gain_ref, f32[1,768]{1,0:T(1,128)} %broadcast_in_dim.74.shift_ref, ...), custom_call_target="tpu_custom_call" | custom-call | flops 14495514624 | bytes 41287680 | tf_op jit(solution)/shard_map/qkv_forward/pallas_call | solution.py:457
  188.9 104.2 %attention_forward.1 = (bf16[4096,768]{1,0:T(8,128)(2,1)}, f32[6,2,4096]{2,1,0:T(2,128)}) custom-call(s32[16]{0:T(128)} %reshape.224.low_ref, s32[2,1,2048]{2,1,0:T(1,128)} %compare_select_fusion.2.start_ref, bf16[4096,768]{1,0:T(8,128)(2,1)} %get-tuple-element.37.q_ref, bf16[4096,768]{1,0:T(8,128)(2,1)} %get-tuple-element.38.k_ref, ...), custom_call_target="tpu_custom_call" | custom-call | flops 12884901888 | bytes 25165824 | tf_op jit(solution)/shard_map/attention_forward/pallas_call | solution.py:542
  293.2 172.7 %feed_forward.1 = (bf16[4096,768]{1,0:T(8,128)(2,1)}, f32[4096,768]{1,0:T(8,128)}, bf16[4096,768]{1,0:T(8,128)(2,1)}, f32[6,2,4096]{2,1,0:T(2,128)}, bf16[768,30...) custom-call(bf16[4096,768]{1,0:T(8,128)(2,1)} %bitcast.14, ...), custom_call_target="tpu_custom_call" | custom-call | flops 130459631616 | bytes 44040192 | tf_op jit(solution)/shard_map/feed_forward/pallas_call | solution.py:737
  465.9 160.7 %attention_backward.1 = (bf16[4096,768]{1,0:T(8,128)(2,1)}, bf16[4096,768]{1,0:T(8,128)(2,1)}, bf16[4096,768]{1,0:T(8,128)(2,1)}) custom-call(s32[16]{0:T(128)} %sub.26.high_ref, s32[2,1,2048]{2,1,0:T(1,128)} %compare_select_fusion.2.start_ref, bf16[4096,768]{1,0:T(8,128)(2,1)} %get-tuple-element.37.q_ref, bf16[4096,768]{1,0:T(8,128)(2,1)} %get-tuple-element.38.k_ref, ...), custom_call_target="tpu_custom_call" | custom-call | flops 32212254720 | bytes 50331648 | tf_op jit(solution)/shard_map/attention_backward/pallas_call | solution.py:634
  626.6 26.7 %qkv_weight_gradient.1 = (bf16[768,2304]{1,0:T(8,128)(2,1)}, f32[16,768]{1,0:T(8,128)}) custom-call(bf16[4096,768]{1,0:T(8,128)(2,1)} %bitcast.15, f32[1,768]{1,0:T(1,128)} %broadcast_in_dim.73.gain_ref, f32[1,768]{1,0:T(1,128)} %broadcast_in_dim.74.shift_ref, bf16[4096,768]{1,0:T(8,128)(2,1)} %get-tuple-element.47.dq_ref, ...), custom_call_target="tpu_custom_call" | custom-call | flops 14495514624 | bytes 25165824 | tf_op jit(solution)/shard_map/qkv_weight_gradient/pallas_call | solution.py:799
  655.4 16.1 %collective-permute-start.3 = (bf16[2,1024,768]{2,1,0:T(8,128)(2,1)S(1)}, bf16[2,1024,768]{2,1,0:T(8,128)(2,1)}, u32[]{:S(2)}, u32[]{:S(2)}) collective-permute-start(bf16[2,1024,768]{2,1,0:T(8,128)(2,1)S(1)} %constant_dynamic-slice_fusion), channel_id=1, source_target_pairs={{0,1},{1,0},{2,3},{3,2},{4,5},{5,4},{6,7},{7,6},{8,9},{9,8},{10,11... | collective-permute-start | bytes 9437192 | tf_op jit(solution)/shard_map/ppermute | solution.py:873
  671.6 27.2 %qkv_input_gradient.1 = (f32[4096,768]{1,0:T(8,128)}, f32[16,768]{1,0:T(8,128)}) custom-call(bf16[4096,768]{1,0:T(8,128)(2,1)} %bitcast.16, f32[1,768]{1,0:T(1,128)} %broadcast_in_dim.73.gain_ref, bf16[768,2304]{1,0:T(8,128)(2,1)} %w_ref.3, bf16[4096,768]{1,0:T(8,128)(2,1)} %get-tuple-element.47.dq_ref, bf16[4096,768]{1,0:T(8,128)(2,1)} %get-tuple-element.48.dk_ref, ...), custom_call_target="tpu_custom_call" | custom-call | flops 14495514624 | bytes 50331648 | tf_op jit(solution)/shard_map/qkv_input_gradient/pallas_call | solution.py:843
  698.7 4.8 dynamic-slice_convert_fusion
  703.7 320.8 %psum.35 = f32[9216]{0:T(1024)S(1)} all-reduce(f32[9216]{0:T(1024)S(1)} %pad_maximum_fusion.4), channel_id=1, replica_groups=mesh['rows'=16,'seq'=2] {'rows','seq'}, use_global_device_ids=true, to_apply=%region_5.6 | all-reduce | flops 9216 | bytes 73728 | tf_op jit(solution)/shard_map/psum | solution.py:918
  1026.3 4.0 broadcast_select_fusion.1
  1030.3 3.2 pad_maximum_fusion.3
  1033.6 10.3 convert_select_fusion.1
  1043.8 10.7 pad_maximum_fusion
  1054.6 81.6 %all-reduce.3.cloned.1.call-done = (bf16[3072,768]{0,1:T(8,128)(2,1)}, bf16[768,2304]{1,0:T(8,128)(2,1)}, bf16[768,768]{1,0:T(8,128)(2,1)}, bf16[768,3072]{1,0:T(8,128)(2,1)}) async-done(((bf16[3072,768]{0,1:T(8,128)(2,1)}, bf16[768,2304]{1,0:T(8,128)(2,1)}, bf16[768,768]{1,0:T(8,128)(2,1)}, bf16[768,3072]{1,0:T(8,128)(2,1)}), (bf16[3072,768]{0,1:T(8,128)(2,1)}, bf16[768,2304]{1,0:T(8,128)(2,1)}, ...) | async-done | bytes 14155792 | tf_op jit(solution)/shard_map/psum | solution.py:908
  1136.2 2.8 convert_element_type.40
  1139.1 7.5 copy.32
  1146.6 3.9 convert_element_type.39
  1151.1 5.0 convert_element_type.41
  (75 shorter events, 17.6 us)
Async XLA Ops:
  7.2 1129.0 %all-reduce.3.cloned.1.call-start = ((), (), s32[]{:S(2)}) async-start(), calls=%async_computation | async-start | bytes 28311552 | tf_op jit(solution)/shard_map/psum | solution.py:908
  7.2 7.0 copy-start
  7.2 9.6 copy-start.7
  7.3 11.6 copy-start.9
  7.3 12.1 %copy-start.10 = (f32[768]{0:T(1024)S(1)}, f32[768]{0:T(1024)}, u32[]{:S(2)}) copy-start(f32[768]{0:T(1024)} %param.18) | copy-start | bytes 9220
  7.3 12.7 %copy-start.11 = (f32[768]{0:T(1024)S(1)}, f32[768]{0:T(1024)}, u32[]{:S(2)}) copy-start(f32[768]{0:T(1024)} %param.22) | copy-start | bytes 9220
  7.3 13.3 %copy-start.12 = (f32[768]{0:T(1024)S(1)}, f32[768]{0:T(1024)}, u32[]{:S(2)}) copy-start(f32[768]{0:T(1024)} %param.23) | copy-start | bytes 9220
  7.3 13.9 %copy-start.13 = (f32[768]{0:T(1024)S(1)}, f32[768]{0:T(1024)}, u32[]{:S(2)}) copy-start(f32[768]{0:T(1024)} %param.24) | copy-start | bytes 9220
  7.3 14.4 %copy-start.14 = (f32[768]{0:T(1024)S(1)}, f32[768]{0:T(1024)}, u32[]{:S(2)}) copy-start(f32[768]{0:T(1024)} %param.28) | copy-start | bytes 9220
  7.3 15.0 %copy-start.8 = (f32[1536]{0:T(1024)S(1)}, f32[1536]{0:T(1024)}, u32[]{:S(2)}) copy-start(f32[1536]{0:T(1024)} %param.20) | copy-start | bytes 18436
  11.2 141.4 %collective-permute-start.2 = (bf16[2,1024,768]{2,1,0:T(8,128)(2,1)}, bf16[2,1024,768]{2,1,0:T(8,128)(2,1)S(1)}, u32[]{:S(2)}, u32[]{:S(2)}) collective-permute-start(bf16[2,1024,768]{2,1,0:T(8,128)(2,1)} %constant_dynamic-slice_fusion.1), channel_id=1, source_target_pairs={{0,1},{1,0},{2,3},{3,2},{4,5},{5,4},{6,7},{7,6},{8,9},{9,8},{10,11... | collective-permute-start | bytes 9437192 | tf_op jit(solution)/shard_map/ppermute | solution.py:862
  16.1 138.2 %collective-permute-start = (bf16[2,1024,768]{2,1,0:T(8,128)(2,1)}, bf16[2,1024,768]{2,1,0:T(8,128)(2,1)}, u32[]{:S(2)}, u32[]{:S(2)}) collective-permute-start(bf16[2,1024,768]{2,1,0:T(8,128)(2,1)} %constant_dynamic-slice_fusion.3), channel_id=1, source_target_pairs={{0,1},{1,0},{2,3},{3,2},{4,5},{5,4},{6,7},{7,6},{8,9},{9,8},{10,11... | collective-permute-start | bytes 9437192 | tf_op jit(solution)/shard_map/ppermute | solution.py:862
  16.8 133.3 %collective-permute-start.1 = (s32[2,1024]{1,0:T(2,128)S(1)}, s32[2,1024]{1,0:T(2,128)S(1)}, u32[]{:S(2)}, u32[]{:S(2)}) collective-permute-start(s32[2,1024]{1,0:T(2,128)S(1)} %constant_dynamic-slice_fusion.2), channel_id=1, source_target_pairs={{0,1},{1,0},{2,3},{3,2},{4,5},{5,4},{6,7},{7,6},{8,9},{9,8},{10,11... | collective-permute-start | bytes 24584 | tf_op jit(solution)/shard_map/ppermute | solution.py:862
  152.6 1.7 copy-start.2
  655.4 370.9 %collective-permute-start.3 = (bf16[2,1024,768]{2,1,0:T(8,128)(2,1)S(1)}, bf16[2,1024,768]{2,1,0:T(8,128)(2,1)}, u32[]{:S(2)}, u32[]{:S(2)}) collective-permute-start(bf16[2,1024,768]{2,1,0:T(8,128)(2,1)S(1)} %constant_dynamic-slice_fusion), channel_id=1, source_target_pairs={{0,1},{1,0},{2,3},{3,2},{4,5},{5,4},{6,7},{7,6},{8,9},{9,8},{10,11... | collective-permute-start | bytes 9437192 | tf_op jit(solution)/shard_map/ppermute | solution.py:873
  698.7 4.9 copy-start.3
  698.7 4.9 copy-start.5
  698.7 4.9 copy-start.6
  698.7 4.9 copy-start.4
  703.6 330.0 %collective-permute-start.4 = (bf16[2,1024,768]{2,1,0:T(8,128)(2,1)}, bf16[2,1024,768]{2,1,0:T(8,128)(2,1)}, u32[]{:S(2)}, u32[]{:S(2)}) collective-permute-start(bf16[2,1024,768]{2,1,0:T(8,128)(2,1)} %dynamic-slice_convert_fusion), channel_id=1, source_target_pairs={{0,1},{1,0},{2,3},{3,2},{4,5},{5,4},{6,7},{7,6},{8,9},{9,8},{10,11... | collective-permute-start | bytes 9437192 | tf_op jit(solution)/shard_map/ppermute | solution.py:873
  1139.1 7.6 copy-start.1
  1146.6 4.0 slice-start
  1146.6 4.5 slice-start.1
Sparse Core Ops, SparseCore 0:
  653.4 482.7 all-reduce.2
